TPU v7x, 32 devices: a whole 2x2x4 slice. The times are simulated.
32 devices in a mesh: gx: 16 (over z, y, x), gy: 2 (over core).
Axes of the slice: x: 2, y: 2, z: 4, core: 2. Of those that a mesh axis runs over, the one named last changes fastest.
Arguments:
- blocks_a: bfloat16 [16, 16, 5, 4096], P('gx', 'gy'), may hold values from -0.75 to 0.75
- prolong: bfloat16 [16, 16, 4096], P('gx', 'gy'), may hold values from -1.5 to 1.5
- aggregate: int32 [16, 16], P('gx', 'gy'), may hold values from 0 to 15, as said below
- coupling_slot: int32 [16, 16, 5], P('gx', 'gy'), may hold values from 0 to 7
Outputs:
- coarse: float32 [16, 2, 8, 4096], P('gx', 'gy')
Inputs may be any that keep to these rules, and one draw needn't show every extreme that they name: The aggregate a of an element is held by the device of gx index a // 1 in the element's own gy column. Of the elements of any one device at most 2 have aggregates held by one gx index, and on every device some gx index holds exactly 2 of them.
All inputs are finite; a program needn't handle non-finite values.
Results may differ from a plain program's by a relative error of at most 0.004.
Values may be sent and summed in bfloat16 or wider, within the bound.
A program may use at most 64 MiB of HBM per device.

v0:
```python
import jax
import jax.numpy as jnp
from jax import lax
from jax.sharding import PartitionSpec as P

B = 64
K = 5
CS = 8
AGG_DEV = 1


def padded_2(block, sides, width):
    for axis, dim in sides:
        count = lax.axis_size(axis)
        forward = [(i, i + 1) for i in range(count - 1)]
        backward = [(target, source) for source, target in forward]
        low = lax.ppermute(
            lax.slice_in_dim(block, block.shape[dim] - width, None, axis=dim), axis, forward
        )
        high = lax.ppermute(lax.slice_in_dim(block, 0, width, axis=dim), axis, backward)
        block = jnp.concatenate([low, block, high], axis=dim)
    return block


def body(blocks_a, prolong, aggregate, coupling_slot):
    grid_rows, grid_cols, block_len = prolong.shape
    elements = grid_rows * grid_cols
    owner_count = lax.axis_size("gx")
    capacity = max(2, 2 * elements // owner_count)
    padded = padded_2(prolong, (("gx", 0), ("gy", 1)), 1)
    beside = jnp.stack(
        [
            padded[1:-1, 1:-1],
            padded[:-2, 1:-1],
            padded[2:, 1:-1],
            padded[1:-1, :-2],
            padded[1:-1, 2:],
        ],
        axis=2,
    )
    matrix_a = blocks_a.reshape(elements, K, B, B)
    matrix_p = beside.reshape(elements, K, B, B)
    product = jnp.einsum(
        "ekab,ekbc->ekac", matrix_a, matrix_p, preferred_element_type=jnp.float32
    ).astype(jnp.bfloat16)
    owners = (aggregate // AGG_DEV).reshape(elements)
    local_id = (aggregate % AGG_DEV).reshape(elements)
    onehot = (owners[:, None] == jnp.arange(owner_count, dtype=jnp.int32)[None, :]).astype(
        jnp.int32
    )
    rank_in = jnp.sum(jnp.cumsum(onehot, axis=0) * onehot, axis=1) - 1
    position = owners * capacity + rank_in
    target = local_id[:, None] * CS + coupling_slot.reshape(elements, K)
    labels = jnp.full((owner_count * capacity, K), -1, jnp.int32).at[position].set(target)
    labels = labels.reshape(owner_count, capacity, K)
    own_block = prolong.reshape(elements, B, B)
    contribution = jnp.einsum(
        "eba,ekbc->ekac", own_block, product, preferred_element_type=jnp.float32
    ).astype(jnp.bfloat16)
    payload = jnp.zeros((owner_count * capacity, K, block_len), jnp.bfloat16)
    payload = payload.at[position].set(contribution.reshape(elements, K, block_len))
    payload = payload.reshape(owner_count, capacity, K, block_len)
    arrived, arrived_tags = (
        lax.all_to_all(payload, "gx", split_axis=0, concat_axis=0, tiled=True),
        lax.all_to_all(labels, "gx", split_axis=0, concat_axis=0, tiled=True),
    )
    arrived_rows = arrived.reshape(-1, block_len)
    flat_tags = arrived_tags.reshape(-1)
    select = (jnp.arange(AGG_DEV * CS, dtype=jnp.int32)[:, None] == flat_tags[None, :]).astype(
        jnp.bfloat16
    )
    coarse = jnp.dot(select, arrived_rows, preferred_element_type=jnp.float32)
    return coarse.reshape(AGG_DEV, 1, CS, block_len)


def solution(mesh):
    return jax.shard_map(
        body,
        mesh=mesh,
        in_specs=(
            P("gx", "gy", None, None),
            P("gx", "gy", None),
            P("gx", "gy"),
            P("gx", "gy", None),
        ),
        out_specs=P("gx", "gy", None, None),
        check_vma=False,
    )
```

profile of v0, /device:TPU:0, one launch (start us, length us, event | category | flops | bytes accessed | tf_op | source)
XLA Modules:
  0.0 71.7 jit_solution(10076009437906470065)
XLA Ops:
  0.0 0.0 copy-start
  0.0 5.0 %collective-permute-start = (bf16[1,8,4096]{2,1,0:T(8,128)(2,1)}, bf16[1,8,4096]{2,1,0:T(8,128)(2,1)S(1)}, u32[]{:S(2)}, u32[]{:S(2)}) collective-permute-start(bf16[1,8,4096]{2,1,0:T(8,128)(2,1)} %param.5), channel_id=1, source_target_pairs={{0,2},{2,4},{4,6},{6,8},{8,10},{10,12},{12,14},{14,16},{16,18},{18... | collective-permute-start | bytes 196616 | tf_op jit(solution)/shard_map/ppermute | solution.py:17
  5.0 1.3 %collective-permute-start.1 = (bf16[1,8,4096]{2,1,0:T(8,128)(2,1)}, bf16[1,8,4096]{2,1,0:T(8,128)(2,1)S(1)}, u32[]{:S(2)}, u32[]{:S(2)}) collective-permute-start(bf16[1,8,4096]{2,1,0:T(8,128)(2,1)} %param.5), channel_id=1, source_target_pairs={{2,0},{4,2},{6,4},{8,6},{10,8},{12,10},{14,12},{16,14},{18,16},{20... | collective-permute-start | bytes 196616 | tf_op jit(solution)/shard_map/ppermute | solution.py:20
  6.3 0.7 %fusion.9 = s32[8,16]{1,0:T(8,128)S(1)} fusion(s32[8]{0:T(128)} %bitcast.36), kind=kLoop, calls=%fused_computation.26 | loop fusion | flops 256 | bytes 544 | tf_op jit(solution)/shard_map/convert_element_type | solution.py:48
  7.0 0.8 %select_reduce_fusion = s32[8]{0:T(128)S(1)} fusion(s32[8,16]{1,0:T(8,128)S(1)} %reduce_window_sum.11, s32[8]{0:T(128)} %bitcast.37), kind=kLoop, calls=%fused_computation.24 | loop fusion | flops 376 | bytes 576 | tf_op jit(solution)/shard_map/reduce_sum | solution.py:51
  7.9 0.7 fusion.10
  8.5 0.8 %copy.32 = s32[1,8,5]{2,1,0:T(8,128)S(1)} copy(s32[1,8,5]{1,0,2:T(1,128)} %param.7) | data formatting | bytes 320 | tf_op args[3]
  9.3 1.2 %scatter_custom_fusion = s32[32,5]{1,0:T(8,128)} fusion(s32[8]{0:T(128)S(1)} %fusion.10, s32[]{:T(128)} %constant.35.clone.1, s32[1,8,5]{2,1,0:T(8,128)S(1)} %copy.32), kind=kCustom, calls=%fused_computation.19 | custom fusion | bytes 4740 | tf_op jit(solution)/shard_map/scatter | solution.py:54
  10.5 8.0 %all-to-all-start = ((s32[16,2,5]{2,1,0:T(2,128)}), s32[16,2,5]{2,1,0:T(2,128)S(1)}, u32[]{:S(2)}, u32[]{:S(2)}) async-start(s32[16,2,5]{2,1,0:T(2,128)} %bitcast.5), calls=%async_computation | async-start | bytes 32768 | tf_op jit(solution)/shard_map/all_to_all | solution.py:65
  18.5 1.0 %stack.18 = bf16[8,1,64,64]{3,2,0,1:T(8,128)(2,1)S(1)} reshape(bf16[1,8,4096]{2,1,0:T(8,128)(2,1)} %param.5) | data formatting | bytes 131072 | tf_op jit(solution)/shard_map/stack | solution.py:31
  19.5 1.0 %reshape.102 = bf16[8,64,64,1]{2,1,0,3:T(8,128)(2,1)S(1)} reshape(bf16[1,8,4096]{2,1,0:T(8,128)(2,1)} %param.5) | data formatting | bytes 131072 | tf_op jit(solution)/shard_map/reshape | solution.py:56
  20.6 0.1 copy.33
  20.7 1.6 %reshape.80 = bf16[8,5,64,64]{3,2,0,1:T(8,128)(2,1)S(1)} reshape(bf16[1,8,5,4096]{3,1,2,0:T(8,128)(2,1)} %param.4) | data formatting | bytes 655360 | tf_op jit(solution)/shard_map/reshape | solution.py:41
  22.3 0.0 collective-permute-done
  22.4 0.0 copy-done
  22.4 0.0 collective-permute-done.1
  22.4 0.1 fusion.11
  22.5 1.3 %collective-permute-start.2 = (bf16[3,1,4096]{2,1,0:T(2,128)(2,1)S(1)}, bf16[3,1,4096]{2,1,0:T(2,128)(2,1)S(1)}, u32[]{:S(2)}, u32[]{:S(2)}) collective-permute-start(bf16[3,1,4096]{2,1,0:T(2,128)(2,1)S(1)} %get-tuple-element.8), channel_id=1, source_target_pairs={{0,1},{2,3},{4,5},{6,7},{8,9},{10,11},{12,13},{14,15},{16,17},{18,... | collective-permute-start | bytes 73736 | tf_op jit(solution)/shard_map/ppermute | solution.py:17
  23.8 1.3 %collective-permute-start.3 = (bf16[3,1,4096]{2,1,0:T(2,128)(2,1)S(1)}, bf16[3,1,4096]{2,1,0:T(2,128)(2,1)S(1)}, u32[]{:S(2)}, u32[]{:S(2)}) collective-permute-start(bf16[3,1,4096]{2,1,0:T(2,128)(2,1)S(1)} %get-tuple-element.7), channel_id=1, source_target_pairs={{1,0},{3,2},{5,4},{7,6},{9,8},{11,10},{13,12},{15,14},{17,16},{19,... | collective-permute-start | bytes 73736 | tf_op jit(solution)/shard_map/ppermute | solution.py:20
  25.1 0.2 stack.19
  25.3 0.1 copy.34
  25.4 0.2 stack.20
  25.6 0.1 copy.35
  25.8 0.0 collective-permute-done.2
  25.8 1.1 %collective-permute-done.3 = bf16[3,1,4096]{2,1,0:T(2,128)(2,1)S(1)} collective-permute-done((bf16[3,1,4096]{2,1,0:T(2,128)(2,1)S(1)}, bf16[3,1,4096]{2,1,0:T(2,128)(2,1)S(1)}, u32[]{:S(2)}, u32[]{:S(2)}) %collective-permute-start.3) | collective-permute-done | bytes 24608 | tf_op jit(solution)/shard_map/ppermute | solution.py:20
  26.9 0.1 pad_maximum_fusion
  27.0 0.2 stack.21
  27.2 0.1 copy.36
  27.3 0.2 stack.22
  27.5 0.1 copy.37
  27.7 0.6 fusion.1
  28.3 0.3 copy.44
  28.6 0.6 reshape.104
  29.2 0.2 broadcast_in_dim.5
  29.4 0.8 %scatter_fusion = bf16[32,5,4096]{2,1,0:T(8,128)(2,1)S(1)} fusion(bf16[32,5,4096]{2,1,0:T(8,128)(2,1)S(1)} %broadcast_in_dim.5, s32[8]{0:T(128)S(1)} %fusion.10, bf16[8,5,4096]{2,1,0:T(8,128)(2,1)S(1)} %reshape.104), kind=kCustom, calls=%fused_computation.1 | custom fusion | bytes 983072 | tf_op jit(solution)/shard_map/scatter | solution.py:61
  30.2 2.6 %copy.41 = bf16[16,2,5,4096]{3,1,2,0:T(2,128)(2,1)} copy(bf16[16,2,5,4096]{3,2,1,0:T(8,128)(2,1)S(1)} %bitcast.35) | data formatting | bytes 2621440 | tf_op jit(solution)/shard_map/reshape | solution.py:62
  32.8 0.0 all-to-all-done
  32.8 6.9 %all-to-all-start.1 = ((bf16[16,2,5,4096]{3,1,2,0:T(2,128)(2,1)}), bf16[16,2,5,4096]{3,1,2,0:T(2,128)(2,1)S(1)}, u32[]{:S(2)}, u32[]{:S(2)}) async-start(bf16[16,2,5,4096]{3,1,2,0:T(2,128)(2,1)} %copy.41), calls=%async_computation.1 | async-start | bytes 2621440 | tf_op jit(solution)/shard_map/all_to_all | solution.py:64
  39.8 0.1 eq.37
  39.9 29.5 %all-to-all-done.1 = bf16[16,2,5,4096]{3,1,2,0:T(2,128)(2,1)S(1)} async-done(((bf16[16,2,5,4096]{3,1,2,0:T(2,128)(2,1)}), bf16[16,2,5,4096]{3,1,2,0:T(2,128)(2,1)S(1)}, u32[]{:S(2)}, u32[]{:S(2)}) %all-to-all-start.1) | async-done | bytes 1310752 | tf_op jit(solution)/shard_map/all_to_all | solution.py:64
  69.3 0.9 %copy.42 = bf16[16,2,5,4096]{3,2,1,0:T(8,128)(2,1)S(1)} copy(bf16[16,2,5,4096]{3,1,2,0:T(2,128)(2,1)S(1)} %all-to-all-done.1) | data formatting | bytes 2621440 | tf_op jit(solution)/shard_map/all_to_all | solution.py:64
  70.2 0.6 reshape.84
  70.8 0.9 %convolution_bitcast_fusion = f32[1,1,8,4096]{3,2,1,0:T(8,128)} fusion(bf16[160,4096]{1,0:T(8,128)(2,1)S(1)} %reshape.84, s32[160]{0:T(256)S(1)} %eq.37), kind=kOutput, calls=%fused_computation.2 | convolution fusion | flops 10487040 | bytes 1442432 | tf_op jit(solution)/shard_map/dot_general | solution.py:72
  (9 shorter events, 0.1 us)
Async XLA Ops:
  0.0 22.4 %copy-start = (bf16[1,8,4096]{2,1,0:T(8,128)(2,1)S(1)}, bf16[1,8,4096]{2,1,0:T(8,128)(2,1)}, u32[]{:S(2)}) copy-start(bf16[1,8,4096]{2,1,0:T(8,128)(2,1)} %param.5) | copy-start | bytes 196612
  0.0 22.3 %collective-permute-start = (bf16[1,8,4096]{2,1,0:T(8,128)(2,1)}, bf16[1,8,4096]{2,1,0:T(8,128)(2,1)S(1)}, u32[]{:S(2)}, u32[]{:S(2)}) collective-permute-start(bf16[1,8,4096]{2,1,0:T(8,128)(2,1)} %param.5), channel_id=1, source_target_pairs={{0,2},{2,4},{4,6},{6,8},{8,10},{10,12},{12,14},{14,16},{16,18},{18... | collective-permute-start | bytes 196616 | tf_op jit(solution)/shard_map/ppermute | solution.py:17
  5.0 17.4 %collective-permute-start.1 = (bf16[1,8,4096]{2,1,0:T(8,128)(2,1)}, bf16[1,8,4096]{2,1,0:T(8,128)(2,1)S(1)}, u32[]{:S(2)}, u32[]{:S(2)}) collective-permute-start(bf16[1,8,4096]{2,1,0:T(8,128)(2,1)} %param.5), channel_id=1, source_target_pairs={{2,0},{4,2},{6,4},{8,6},{10,8},{12,10},{14,12},{16,14},{18,16},{20... | collective-permute-start | bytes 196616 | tf_op jit(solution)/shard_map/ppermute | solution.py:20
  10.5 22.4 %all-to-all-start = ((s32[16,2,5]{2,1,0:T(2,128)}), s32[16,2,5]{2,1,0:T(2,128)S(1)}, u32[]{:S(2)}, u32[]{:S(2)}) async-start(s32[16,2,5]{2,1,0:T(2,128)} %bitcast.5), calls=%async_computation | async-start | bytes 32768 | tf_op jit(solution)/shard_map/all_to_all | solution.py:65
  22.5 3.3 %collective-permute-start.2 = (bf16[3,1,4096]{2,1,0:T(2,128)(2,1)S(1)}, bf16[3,1,4096]{2,1,0:T(2,128)(2,1)S(1)}, u32[]{:S(2)}, u32[]{:S(2)}) collective-permute-start(bf16[3,1,4096]{2,1,0:T(2,128)(2,1)S(1)} %get-tuple-element.8), channel_id=1, source_target_pairs={{0,1},{2,3},{4,5},{6,7},{8,9},{10,11},{12,13},{14,15},{16,17},{18,... | collective-permute-start | bytes 73736 | tf_op jit(solution)/shard_map/ppermute | solution.py:17
  23.8 3.1 %collective-permute-start.3 = (bf16[3,1,4096]{2,1,0:T(2,128)(2,1)S(1)}, bf16[3,1,4096]{2,1,0:T(2,128)(2,1)S(1)}, u32[]{:S(2)}, u32[]{:S(2)}) collective-permute-start(bf16[3,1,4096]{2,1,0:T(2,128)(2,1)S(1)} %get-tuple-element.7), channel_id=1, source_target_pairs={{1,0},{3,2},{5,4},{7,6},{9,8},{11,10},{13,12},{15,14},{17,16},{19,... | collective-permute-start | bytes 73736 | tf_op jit(solution)/shard_map/ppermute | solution.py:20
  32.8 36.5 %all-to-all-start.1 = ((bf16[16,2,5,4096]{3,1,2,0:T(2,128)(2,1)}), bf16[16,2,5,4096]{3,1,2,0:T(2,128)(2,1)S(1)}, u32[]{:S(2)}, u32[]{:S(2)}) async-start(bf16[16,2,5,4096]{3,1,2,0:T(2,128)(2,1)} %copy.41), calls=%async_computation.1 | async-start | bytes 2621440 | tf_op jit(solution)/shard_map/all_to_all | solution.py:64
where the time goes:
time: 73.2 us; the launch traced here: 71.7 us
  waiting for transfers between devices  30.6 us (42%)
  starting transfers between devices  23.8 us (33%)
  local copies, waits for them, and re-layouts  13.2 us (18%)
  other arithmetic  2.32 us (3%)
  matrix products  1.59 us (2%)
    all_to_all x1, waiting for transfers between devices, body(): lax.all_to_all(payload, 'gx', split_axis=0, concat_axis=0, tiled=True)  29.5 us
    all_to_all x1, starting transfers between devices, body(): lax.all_to_all(labels, 'gx', split_axis=0, concat_axis=0, tiled=True)  8.02 us
    all_to_all x1, starting transfers between devices, body(): lax.all_to_all(payload, 'gx', split_axis=0, concat_axis=0, tiled=True)  6.91 us
    ppermute x2, starting transfers between devices, padded_2(): lax.ppermute(lax.slice_in_dim(block, block.shape[dim] - width, None, axis...  6.26 us
    reshape x1, local copies, waits for them, and re-layouts, body(): payload = payload.reshape(owner_count, capacity, K, block_len)  2.61 us
    ppermute x2, starting transfers between devices, padded_2(): lax.ppermute(lax.slice_in_dim(block, 0, width, axis=dim), axis, backward)  2.58 us
    another operation x11, local copies, waits for them, and re-layouts, body(): jnp.stack([padded[1:-1, 1:-1], padded[:-2, 1:-1], padded[2:, 1:-1], padde...  2.4 us
    reshape x1, local copies, waits for them, and re-layouts, body(): matrix_a = blocks_a.reshape(elements, K, B, B)  1.62 us
  transfers between devices with their start and end apart: 6, of which 2 were waited for; matrix products, arithmetic and copies ran while one was open for 20% of the time, Pallas kernels for 0%

commit v1 on v0

v1 whole, which is shorter than its diff:
```python
import functools

import jax
import jax.numpy as jnp
from jax import lax
from jax.experimental import pallas as pl
from jax.experimental.pallas import tpu as pltpu
from jax.sharding import PartitionSpec as P

B = 64
K = 5
CS = 8
MESH = pl.DeviceIdType.MESH


def neighbours(block, axis, dim):
    count = lax.axis_size(axis)
    forward = [(i, i + 1) for i in range(count - 1)]
    backward = [(target, source) for source, target in forward]
    last = lax.slice_in_dim(block, block.shape[dim] - 1, None, axis=dim)
    first = lax.slice_in_dim(block, 0, 1, axis=dim)
    low = lax.ppermute(last, axis, forward)
    high = lax.ppermute(first, axis, backward)
    return low, high


def bit_orders(n):
    bits = [1 << i for i in range(n.bit_length() - 1)]
    swapped = list(bits)
    for i in range(0, len(bits) - 1, 2):
        swapped[i], swapped[i + 1] = bits[i + 1], bits[i]
    return bits, swapped


def places(order):
    offsets = [0]
    for bit in reversed(order):
        offsets = offsets + [o | bit for o in offsets]
    return offsets


def exchange(n, orders, select_ref, rows_ref, out_ref, acc, *rest):
    steps = len(orders[0])
    send, recv = rest[:steps], rest[steps : 2 * steps]
    send_sem, recv_sem = rest[2 * steps :]
    me = lax.axis_index("gx")

    def partner(bit):
        return me + bit - 2 * bit * ((me // bit) % 2)

    barrier = pltpu.get_barrier_semaphore()
    for bit in orders[0]:
        pl.semaphore_signal(
            barrier, inc=1, device_id={"gx": partner(bit)}, device_id_type=MESH
        )

    width = rows_ref.shape[1] // 4

    def gathered(chain, low, high):
        select = select_ref[chain, low * CS : high * CS, :]
        parts = []
        for q in range(2):
            begin = (chain * 2 + q) * width
            part = jnp.dot(
                select, rows_ref[:, begin : begin + width], preferred_element_type=jnp.float32
            )
            parts.append(part.reshape(high - low, CS, width))
        return jnp.concatenate(parts, axis=1)

    def copy(chain, step):
        return pltpu.make_async_remote_copy(
            src_ref=send[step].at[chain],
            dst_ref=recv[step].at[chain],
            send_sem=send_sem.at[chain, step],
            recv_sem=recv_sem.at[chain, step],
            device_id={"gx": partner(orders[chain][step])},
            device_id_type=MESH,
        )

    half = n // 2
    for chain in range(2):
        send[0][chain] = gathered(chain, half, n).astype(jnp.bfloat16)
        if chain == 0:
            pl.semaphore_wait(barrier, steps)
        copy(chain, 0).start()
    for chain in range(2):
        acc[chain] = gathered(chain, 0, half)
    for step in range(steps):
        count = half >> step
        for chain in range(2):
            copy(chain, step).wait_recv()
            if step + 1 < steps:
                keep = count // 2
                send[step + 1][chain] = (
                    acc[chain, keep:count] + recv[step][chain, keep:count].astype(jnp.float32)
                ).astype(jnp.bfloat16)
                copy(chain, step + 1).start()
                acc[chain, 0:keep] = acc[chain, 0:keep] + recv[step][chain, 0:keep].astype(
                    jnp.float32
                )
            else:
                total = acc[chain, 0] + recv[step][chain, 0].astype(jnp.float32)
                for q in range(2):
                    begin = (chain * 2 + q) * width
                    out_ref[:, begin : begin + width] = total[q * CS : (q + 1) * CS, :]
    for step in range(steps):
        for chain in range(2):
            copy(chain, step).wait_send()


def body(blocks_a, prolong, aggregate, coupling_slot):
    grid_rows, grid_cols, block_len = prolong.shape
    elements = grid_rows * grid_cols
    n = lax.axis_size("gx")
    low_x, high_x = neighbours(prolong, "gx", 0)
    low_y, high_y = neighbours(prolong, "gy", 1)
    beside = jnp.stack(
        [
            prolong,
            jnp.concatenate([low_x, prolong[:-1]], axis=0),
            jnp.concatenate([prolong[1:], high_x], axis=0),
            jnp.concatenate([low_y, prolong[:, :-1]], axis=1),
            jnp.concatenate([prolong[:, 1:], high_y], axis=1),
        ],
        axis=2,
    )
    matrix_a = blocks_a.reshape(elements, K, B, B)
    matrix_p = beside.reshape(elements, K, B, B)
    product = jnp.einsum(
        "ekab,ekbc->ekac", matrix_a, matrix_p, preferred_element_type=jnp.float32
    ).astype(jnp.bfloat16)
    own_block = prolong.reshape(elements, B, B)
    contribution = jnp.einsum(
        "eba,ekbc->ekac", own_block, product, preferred_element_type=jnp.float32
    ).astype(jnp.bfloat16)
    rows = contribution.reshape(elements * K, block_len)

    orders = bit_orders(n)
    steps = len(orders[0])
    me = lax.axis_index("gx")
    offsets = jnp.asarray([places(order) for order in orders], jnp.int32)
    owner_at = jnp.bitwise_xor(offsets, me)
    wanted = owner_at[:, :, None] * CS + jnp.arange(CS, dtype=jnp.int32)[None, None, :]
    target = (aggregate.reshape(elements, 1) * CS + coupling_slot.reshape(elements, K)).reshape(-1)
    select = (wanted.reshape(2, n * CS, 1) == target[None, None, :]).astype(jnp.bfloat16)

    width = block_len // 4
    slots = [(2, n >> (step + 1), 2 * CS, width) for step in range(steps)]
    vmem = pl.BlockSpec(memory_space=pltpu.VMEM)
    coarse = pl.pallas_call(
        functools.partial(exchange, n, orders),
        out_shape=jax.ShapeDtypeStruct((CS, block_len), jnp.float32),
        in_specs=[vmem, vmem],
        out_specs=vmem,
        scratch_shapes=[pltpu.VMEM(slots[0], jnp.float32)]
        + [pltpu.VMEM(shape, jnp.bfloat16) for shape in slots + slots]
        + [pltpu.SemaphoreType.DMA((2, steps)), pltpu.SemaphoreType.DMA((2, steps))],
        compiler_params=pltpu.CompilerParams(
            collective_id=0, has_side_effects=True, vmem_limit_bytes=40 * 1024 * 1024
        ),
    )(select, rows)
    return coarse.reshape(1, 1, CS, block_len)


def solution(mesh):
    return jax.shard_map(
        body,
        mesh=mesh,
        in_specs=(
            P("gx", "gy", None, None),
            P("gx", "gy", None),
            P("gx", "gy"),
            P("gx", "gy", None),
        ),
        out_specs=P("gx", "gy", None, None),
        check_vma=False,
    )
```

time: 73.2 us -> 45.6 us (0.62); the launches traced: 71.7 us -> 45.2 us
  waiting for transfers between devices: 30.6 us -> 0.01 us
  Pallas kernels: 0 us -> 26.4 us
  starting transfers between devices: 23.8 us -> 9.01 us
  local copies, waits for them, and re-layouts: 13.2 us -> 7.35 us
  matrix products: 1.59 us -> 0.7 us
  other arithmetic: 2.32 us -> 1.53 us
    all_to_all x2 -> x0, waiting for transfers between devices: 29.5 us -> none  [the longest x1 29.5 us: body(): lax.all_to_all(payload, 'gx', split_axis=0, concat_axis=0, tiled=True)]
    pallas_call x0 -> x1, Pallas kernels: none -> 26.4 us  [body(): pl.pallas_call(functools.partial(exchange, n, orders), out_shape=jax.Shap...]
    all_to_all x2 -> x0, starting transfers between devices: 14.9 us -> none  [the longest x1 8.02 us: body(): lax.all_to_all(labels, 'gx', split_axis=0, concat_axis=0, tiled=True)]
    reshape x4 -> x2, local copies, waits for them, and re-layouts: 4.07 us -> 0.61 us  [the longest x1 0.53 us: body(): rows = contribution.reshape(elements * K, block_len)]
    scatter x2 -> x0, local copies, waits for them, and re-layouts: 1.96 us -> none  [the longest x1 1.17 us: body(): jnp.full((owner_count * capacity, K), -1, jnp.int32).at[position]]
    slice x1 -> x2, local copies, waits for them, and re-layouts: 0.07 us -> 1.88 us  [the longest x1 0.95 us: neighbours(): first = lax.slice_in_dim(block, 0, 1, axis=dim)]
    mul x0 -> x2, other arithmetic: none -> 1.35 us  [the longest x1 0.69 us: body(): owner_at[:, :, None] * CS + jnp.arange(CS, dtype=jnp.int32)[None, None, :]]
    ppermute x4, waiting for transfers between devices: 1.13 us -> 0.01 us  [the longest x2 0.01 us: neighbours(): high = lax.ppermute(first, axis, backward)]
  transfers between devices with their start and end apart: 6 -> 4, of which waited for: 2 -> 0; matrix products, arithmetic and copies ran while one was open for 20% -> 16% of each run, Pallas kernels for 0% -> 0%
where the time goes in v1:
time: 45.6 us; the launch traced here: 45.2 us
  Pallas kernels  26.4 us (58%)
  starting transfers between devices  9.01 us (20%)
  local copies, waits for them, and re-layouts  7.35 us (16%)
  other arithmetic  1.53 us (3%)
  matrix products  0.7 us (2%)
    pallas_call x1, Pallas kernels, body(): pl.pallas_call(functools.partial(exchange, n, orders), out_shape=jax.Shap...  26.4 us
    ppermute x2, starting transfers between devices, neighbours(): low = lax.ppermute(last, axis, forward)  6.43 us
    ppermute x2, starting transfers between devices, neighbours(): high = lax.ppermute(first, axis, backward)  2.58 us
    another operation x6, local copies, waits for them, and re-layouts, body(): jnp.stack([prolong, jnp.concatenate([low_x, prolong[:-1]], axis=0), jnp.c...  1.75 us
    unnamed x10, local copies, waits for them, and re-layouts  1.49 us
    slice x1, local copies, waits for them, and re-layouts, neighbours(): first = lax.slice_in_dim(block, 0, 1, axis=dim)  0.95 us
    slice x1, local copies, waits for them, and re-layouts, body(): prolong[:, 1:]  0.94 us
  transfers between devices with their start and end apart: 4, of which 0 were waited for; matrix products, arithmetic and copies ran while one was open for 16% of the time, Pallas kernels for 0%

profile of v1, /device:TPU:0, one launch (start us, length us, event | category | flops | bytes accessed | tf_op | source)
XLA Modules:
  0.0 45.2 jit_solution(9606059633884047685)
XLA Ops:
  0.0 0.0 copy-start
  0.0 0.0 copy-start.1
  0.0 5.0 %collective-permute-start = (bf16[1,8,4096]{2,1,0:T(8,128)(2,1)}, bf16[1,8,4096]{2,1,0:T(8,128)(2,1)S(1)}, u32[]{:S(2)}, u32[]{:S(2)}) collective-permute-start(bf16[1,8,4096]{2,1,0:T(8,128)(2,1)} %param.6), channel_id=1, source_target_pairs={{0,2},{2,4},{4,6},{6,8},{8,10},{10,12},{12,14},{14,16},{16,18},{18... | collective-permute-start | bytes 196616 | tf_op jit(solution)/shard_map/ppermute | solution.py:22
  5.0 1.3 %collective-permute-start.1 = (bf16[1,8,4096]{2,1,0:T(8,128)(2,1)}, bf16[1,8,4096]{2,1,0:T(8,128)(2,1)S(1)}, u32[]{:S(2)}, u32[]{:S(2)}) collective-permute-start(bf16[1,8,4096]{2,1,0:T(8,128)(2,1)} %param.6), channel_id=1, source_target_pairs={{2,0},{4,2},{6,4},{8,6},{10,8},{12,10},{14,12},{16,14},{18,16},{20... | collective-permute-start | bytes 196616 | tf_op jit(solution)/shard_map/ppermute | solution.py:23
  6.3 0.9 %fusion.8 = (bf16[1,1,4096]{2,1,0:T(2,128)(2,1)S(1)}, bf16[1,1,4096]{2,1,0:T(2,128)(2,1)S(1)}) fusion(bf16[1,8,4096]{2,1,0:T(8,128)(2,1)} %param.6), kind=kLoop, calls=%fused_computation.19 | loop fusion | bytes 32768 | tf_op jit(solution)/shard_map/slice | solution.py:21
  7.2 1.5 %collective-permute-start.2 = (bf16[1,1,4096]{2,1,0:T(2,128)(2,1)S(1)}, bf16[1,1,4096]{2,1,0:T(2,128)(2,1)S(1)}, u32[]{:S(2)}, u32[]{:S(2)}) collective-permute-start(bf16[1,1,4096]{2,1,0:T(2,128)(2,1)S(1)} %get-tuple-element.8), channel_id=1, source_target_pairs={{0,1},{2,3},{4,5},{6,7},{8,9},{10,11},{12,13},{14,15},{16,17},{18,... | collective-permute-start | bytes 24584 | tf_op jit(solution)/shard_map/ppermute | solution.py:22
  8.7 1.3 %collective-permute-start.3 = (bf16[1,1,4096]{2,1,0:T(2,128)(2,1)S(1)}, bf16[1,1,4096]{2,1,0:T(2,128)(2,1)S(1)}, u32[]{:S(2)}, u32[]{:S(2)}) collective-permute-start(bf16[1,1,4096]{2,1,0:T(2,128)(2,1)S(1)} %get-tuple-element.7), channel_id=1, source_target_pairs={{1,0},{3,2},{5,4},{7,6},{9,8},{11,10},{13,12},{15,14},{17,16},{19,... | collective-permute-start | bytes 24584 | tf_op jit(solution)/shard_map/ppermute | solution.py:23
  10.0 0.9 %fusion.7 = (bf16[1,7,4096]{2,1,0:T(8,128)(2,1)S(1)}, bf16[1,7,4096]{2,1,0:T(8,128)(2,1)S(1)}) fusion(bf16[1,8,4096]{2,1,0:T(8,128)(2,1)} %param.6), kind=kLoop, calls=%fused_computation.18 | loop fusion | bytes 229376 | tf_op jit(solution)/shard_map/slice | solution.py:123
  10.9 1.0 %stack.18 = bf16[8,1,64,64]{3,2,0,1:T(8,128)(2,1)S(1)} reshape(bf16[1,8,4096]{2,1,0:T(8,128)(2,1)} %param.6) | data formatting | bytes 131072 | tf_op jit(solution)/shard_map/stack | solution.py:117
  12.0 0.7 %xor_multiply_fusion = s32[2,16]{1,0:T(2,128)S(1)} fusion(s32[2,16]{1,0:T(2,128)} %constant.11.clone, s32[]{:T(128)S(6)} %axis_index.15), kind=kLoop, calls=%fused_computation.15 | loop fusion | flops 64 | bytes 260 | tf_op jit(solution)/shard_map/mul | solution.py:143
  12.7 0.1 add.37
  12.7 0.1 add.38
  12.8 0.1 add.40
  12.9 0.7 %multiply_bitcast_fusion = s32[8]{0:T(128)S(1)} fusion(s32[1,8]{1,0:T(1,128)} %param.7), kind=kLoop, calls=%fused_computation.16 | loop fusion | flops 8 | bytes 64 | tf_op jit(solution)/shard_map/mul | solution.py:144
  13.6 0.1 add.43
  13.7 0.1 add.44
  13.7 0.8 %copy.8 = s32[1,8,5]{2,1,0:T(8,128)S(1)} copy(s32[1,8,5]{1,0,2:T(1,128)} %param.8) | data formatting | bytes 320 | tf_op args[3]
  14.5 0.1 reshape.64
  14.6 0.1 compare_convert_fusion.select_ref
  14.7 0.0 copy-done
  14.7 0.2 reshape.69
  14.9 0.0 copy-done.1
  14.9 0.7 %reshape.65 = bf16[8,5,64,64]{3,2,0,1:T(8,128)(2,1)S(1)} reshape(bf16[1,8,5,4096]{3,1,2,0:T(8,128)(2,1)S(1)} %copy-done.1) | data formatting | bytes 655360 | tf_op jit(solution)/shard_map/reshape | solution.py:127
  15.6 0.0 collective-permute-done.2
  15.7 0.0 collective-permute-done.3
  15.8 0.2 stack.21
  15.9 0.2 stack.22
  16.1 0.0 collective-permute-done
  16.1 0.2 stack.19
  16.3 0.0 collective-permute-done.1
  16.4 0.2 stack.20
  16.6 0.7 %fusion.1 = bf16[8,5,64,64]{2,3,1,0:T(8,128)(2,1)S(1)} fusion(bf16[8,5,64,64]{3,2,0,1:T(8,128)(2,1)S(1)} %reshape.65, bf16[8,5,64,64]{3,2,0,1:T(8,128)(2,1)S(1)} %constant_dynamic-update-slice_fusion, bf16[8,64,64,1]{2,1,0,3:T(8,128)(2,1)S(1)} %reshape.69), kind=kOutput, calls=%fused_computation.3 | convolution fusion | flops 42270720 | bytes 1048576 | tf_op jit(solution)/shard_map/eba,ekbc->ekac/dot_general | solution.py:133
  17.3 0.3 copy.9
  17.6 0.5 %reshape.67.rows_ref = bf16[40,4096]{1,0:T(8,128)(2,1)S(1)} reshape(bf16[8,5,64,64]{3,2,1,0:T(8,128)(2,1)S(1)} %copy.9) | data formatting | bytes 655360 | tf_op jit(solution)/shard_map/reshape | solution.py:136
  18.2 26.4 %shard_map.55 = f32[8,4096]{1,0:T(8,128)S(1)} custom-call(bf16[2,128,40]{2,1,0:T(8,128)(2,1)S(1)} %compare_convert_fusion.select_ref, bf16[40,4096]{1,0:T(8,128)(2,1)S(1)} %reshape.67.rows_ref), custom_call_target="tpu_custom_call" | custom-call | tf_op jit(solution)/shard_map/pallas_call | solution.py:150
  44.6 0.7 %copy.24 = f32[1,1,8,4096]{3,2,1,0:T(8,128)} copy(f32[1,1,8,4096]{3,2,1,0:T(8,128)S(1)} %bitcast.20) | data formatting | bytes 262144
  (10 shorter events, 0.2 us)
Async XLA Ops:
  0.0 14.7 %copy-start = (bf16[1,8,4096]{2,1,0:T(8,128)(2,1)S(1)}, bf16[1,8,4096]{2,1,0:T(8,128)(2,1)}, u32[]{:S(2)}) copy-start(bf16[1,8,4096]{2,1,0:T(8,128)(2,1)} %param.6) | copy-start | bytes 196612
  0.0 14.9 %copy-start.1 = (bf16[1,8,5,4096]{3,1,2,0:T(8,128)(2,1)S(1)}, bf16[1,8,5,4096]{3,1,2,0:T(8,128)(2,1)}, u32[]{:S(2)}) copy-start(bf16[1,8,5,4096]{3,1,2,0:T(8,128)(2,1)} %param.5) | copy-start | bytes 983044
  0.0 16.1 %collective-permute-start = (bf16[1,8,4096]{2,1,0:T(8,128)(2,1)}, bf16[1,8,4096]{2,1,0:T(8,128)(2,1)S(1)}, u32[]{:S(2)}, u32[]{:S(2)}) collective-permute-start(bf16[1,8,4096]{2,1,0:T(8,128)(2,1)} %param.6), channel_id=1, source_target_pairs={{0,2},{2,4},{4,6},{6,8},{8,10},{10,12},{12,14},{14,16},{16,18},{18... | collective-permute-start | bytes 196616 | tf_op jit(solution)/shard_map/ppermute | solution.py:22
  5.0 11.4 %collective-permute-start.1 = (bf16[1,8,4096]{2,1,0:T(8,128)(2,1)}, bf16[1,8,4096]{2,1,0:T(8,128)(2,1)S(1)}, u32[]{:S(2)}, u32[]{:S(2)}) collective-permute-start(bf16[1,8,4096]{2,1,0:T(8,128)(2,1)} %param.6), channel_id=1, source_target_pairs={{2,0},{4,2},{6,4},{8,6},{10,8},{12,10},{14,12},{16,14},{18,16},{20... | collective-permute-start | bytes 196616 | tf_op jit(solution)/shard_map/ppermute | solution.py:23
  7.2 8.4 %collective-permute-start.2 = (bf16[1,1,4096]{2,1,0:T(2,128)(2,1)S(1)}, bf16[1,1,4096]{2,1,0:T(2,128)(2,1)S(1)}, u32[]{:S(2)}, u32[]{:S(2)}) collective-permute-start(bf16[1,1,4096]{2,1,0:T(2,128)(2,1)S(1)} %get-tuple-element.8), channel_id=1, source_target_pairs={{0,1},{2,3},{4,5},{6,7},{8,9},{10,11},{12,13},{14,15},{16,17},{18,... | collective-permute-start | bytes 24584 | tf_op jit(solution)/shard_map/ppermute | solution.py:22
  8.7 7.0 %collective-permute-start.3 = (bf16[1,1,4096]{2,1,0:T(2,128)(2,1)S(1)}, bf16[1,1,4096]{2,1,0:T(2,128)(2,1)S(1)}, u32[]{:S(2)}, u32[]{:S(2)}) collective-permute-start(bf16[1,1,4096]{2,1,0:T(2,128)(2,1)S(1)} %get-tuple-element.7), channel_id=1, source_target_pairs={{1,0},{3,2},{5,4},{7,6},{9,8},{11,10},{13,12},{15,14},{17,16},{19,... | collective-permute-start | bytes 24584 | tf_op jit(solution)/shard_map/ppermute | solution.py:23

commit v2 on v1

v2 whole, which is shorter than its diff:
```python
import functools

import jax
import jax.numpy as jnp
from jax import lax
from jax.experimental import pallas as pl
from jax.experimental.pallas import tpu as pltpu
from jax.sharding import PartitionSpec as P

B = 64
K = 5
CS = 8
MESH = pl.DeviceIdType.MESH


def bit_orders(n):
    bits = [1 << i for i in range(n.bit_length() - 1)]
    swapped = list(bits)
    for i in range(0, len(bits) - 1, 2):
        swapped[i], swapped[i + 1] = bits[i + 1], bits[i]
    return bits, swapped


def places(order):
    offsets = [0]
    for bit in reversed(order):
        offsets = offsets + [o | bit for o in offsets]
    return offsets


def coarsen(
    n, ny, orders, owner_ref, slot_ref, a_ref, p_ref, out_ref,
    low_x, high_x, low_y, high_y, sums, parts, acc, *rest,
):
    steps = len(orders[0])
    send, recv = rest[:steps], rest[steps : 2 * steps]
    send_sem, recv_sem, halo_send, halo_recv = rest[2 * steps :]
    me, column = lax.axis_index("gx"), lax.axis_index("gy")
    elements = p_ref.shape[0]

    def partner(bit):
        return me + bit - 2 * bit * ((me // bit) % 2)

    sides = [
        (me < n - 1, me > 0, {"gx": jnp.minimum(me + 1, n - 1)}, p_ref, low_x),
        (me > 0, me < n - 1, {"gx": jnp.maximum(me - 1, 0)}, p_ref, high_x),
        (column < ny - 1, column > 0, {"gy": jnp.minimum(column + 1, ny - 1)},
         p_ref.at[elements - 1], low_y),
        (column > 0, column < ny - 1, {"gy": jnp.maximum(column - 1, 0)}, p_ref.at[0], high_y),
    ]

    def halo(i):
        return pltpu.make_async_remote_copy(
            src_ref=sides[i][3], dst_ref=sides[i][4],
            send_sem=halo_send.at[i], recv_sem=halo_recv.at[i],
            device_id=sides[i][2], device_id_type=MESH,
        )

    barrier = pltpu.get_barrier_semaphore()
    for bit in orders[0]:
        pl.semaphore_signal(
            barrier, inc=1, device_id={"gx": partner(bit)}, device_id_type=MESH
        )
    for sends, _, target, _, _ in sides:
        @pl.when(sends)
        def _():
            pl.semaphore_signal(barrier, inc=1, device_id=target, device_id_type=MESH)
    expected = steps
    for sends, _, _, _, _ in sides:
        expected = expected + jnp.where(sends, 1, 0)
    pl.semaphore_wait(barrier, expected)
    for i, (sends, receives, _, _, place) in enumerate(sides):
        @pl.when(sends)
        def _():
            halo(i).start()

        @pl.when(jnp.logical_not(receives))
        def _():
            place[...] = jnp.zeros_like(place)
    for i in range(4):
        @pl.when(sides[i][1])
        def _():
            halo(i).wait_recv()

    for e in range(elements):
        beside = [
            p_ref[e], low_x[e], high_x[e],
            p_ref[e - 1] if e else low_y[...],
            p_ref[e + 1] if e + 1 < elements else high_y[...],
        ]
        products = [
            jnp.dot(a_ref[e * K + k], beside[k], preferred_element_type=jnp.float32)
            .astype(jnp.bfloat16).astype(jnp.float32)
            for k in range(K)
        ]
        for s in range(CS):
            total = products[0] * slot_ref[(e * K) * CS + s]
            for k in range(1, K):
                total = total + products[k] * slot_ref[(e * K + k) * CS + s]
            sums[e % 2, :, s * B : (s + 1) * B] = total.astype(jnp.bfloat16)
        parts[e] = (
            lax.dot_general(
                p_ref[e], sums[e % 2], (((0,), (0,)), ((), ())),
                preferred_element_type=jnp.float32,
            ).astype(jnp.bfloat16).astype(jnp.float32)
        )

    rows = B // 2

    def gathered(chain, place):
        base = (chain * n + place) * elements
        total = parts[0, chain * rows : (chain + 1) * rows, :] * owner_ref[base]
        for e in range(1, elements):
            total = total + parts[e, chain * rows : (chain + 1) * rows, :] * owner_ref[base + e]
        return total

    def copy(chain, step):
        return pltpu.make_async_remote_copy(
            src_ref=send[step].at[chain],
            dst_ref=recv[step].at[chain],
            send_sem=send_sem.at[chain, step],
            recv_sem=recv_sem.at[chain, step],
            device_id={"gx": partner(orders[chain][step])},
            device_id_type=MESH,
        )

    half = n // 2
    for chain in range(2):
        @pl.loop(0, half)
        def _(p):
            send[0][chain, p] = gathered(chain, half + p).astype(jnp.bfloat16)

        copy(chain, 0).start()
    for chain in range(2):
        @pl.loop(0, half)
        def _(p):
            acc[chain, p] = gathered(chain, p)

    for step in range(steps):
        count = half >> step
        for chain in range(2):
            copy(chain, step).wait_recv()
            if step + 1 < steps:
                keep = count // 2
                send[step + 1][chain] = (
                    acc[chain, keep:count] + recv[step][chain, keep:count].astype(jnp.float32)
                ).astype(jnp.bfloat16)
                copy(chain, step + 1).start()
                acc[chain, 0:keep] = acc[chain, 0:keep] + recv[step][chain, 0:keep].astype(
                    jnp.float32
                )
            else:
                out_ref[chain * rows : (chain + 1) * rows, :] = acc[chain, 0] + recv[step][
                    chain, 0
                ].astype(jnp.float32)
    for step in range(steps):
        for chain in range(2):
            copy(chain, step).wait_send()
    for i in range(4):
        @pl.when(sides[i][0])
        def _():
            halo(i).wait_send()


def body(blocks_a, prolong, aggregate, coupling_slot):
    grid_rows, grid_cols, block_len = prolong.shape
    elements = grid_rows * grid_cols
    n, ny = lax.axis_size("gx"), lax.axis_size("gy")
    matrix_a = blocks_a.reshape(elements * K, B, B)
    matrix_p = prolong.reshape(elements, B, B)

    orders = bit_orders(n)
    steps = len(orders[0])
    offsets = jnp.asarray([places(order) for order in orders], jnp.int32)
    owner_at = jnp.bitwise_xor(offsets, lax.axis_index("gx"))
    owners = aggregate.reshape(elements)
    owner_is = (owner_at[:, :, None] == owners[None, None, :]).astype(jnp.float32).reshape(-1)
    slots = coupling_slot.reshape(elements * K, 1)
    slot_is = (slots == jnp.arange(CS, dtype=jnp.int32)[None, :]).astype(jnp.float32).reshape(-1)

    places_of = [(2, n >> (step + 1), B // 2, CS * B) for step in range(steps)]
    vmem = pl.BlockSpec(memory_space=pltpu.VMEM)
    smem = pl.BlockSpec(memory_space=pltpu.SMEM)
    coarse = pl.pallas_call(
        functools.partial(coarsen, n, ny, orders),
        out_shape=jax.ShapeDtypeStruct((B, CS * B), jnp.float32),
        in_specs=[smem, smem, vmem, vmem],
        out_specs=vmem,
        scratch_shapes=[
            pltpu.VMEM((elements, B, B), jnp.bfloat16),
            pltpu.VMEM((elements, B, B), jnp.bfloat16),
            pltpu.VMEM((B, B), jnp.bfloat16),
            pltpu.VMEM((B, B), jnp.bfloat16),
            pltpu.VMEM((2, B, CS * B), jnp.bfloat16),
            pltpu.VMEM((elements, B, CS * B), jnp.float32),
            pltpu.VMEM(places_of[0], jnp.float32),
        ]
        + [pltpu.VMEM(shape, jnp.bfloat16) for shape in places_of + places_of]
        + [
            pltpu.SemaphoreType.DMA((2, steps)),
            pltpu.SemaphoreType.DMA((2, steps)),
            pltpu.SemaphoreType.DMA((4,)),
            pltpu.SemaphoreType.DMA((4,)),
        ],
        compiler_params=pltpu.CompilerParams(
            collective_id=0, has_side_effects=True, vmem_limit_bytes=40 * 1024 * 1024
        ),
    )(owner_is, slot_is, matrix_a, matrix_p)
    coarse = coarse.reshape(B, CS, B).transpose(1, 0, 2)
    return coarse.reshape(1, 1, CS, block_len)


def solution(mesh):
    return jax.shard_map(
        body,
        mesh=mesh,
        in_specs=(
            P("gx", "gy", None, None),
            P("gx", "gy", None),
            P("gx", "gy"),
            P("gx", "gy", None),
        ),
        out_specs=P("gx", "gy", None, None),
        check_vma=False,
    )
```

time: 45.6 us -> 39.4 us (0.86)
  starting transfers between devices: 9.01 us -> 0 us
  Pallas kernels: 26.4 us -> 33.7 us
  local copies, waits for them, and re-layouts: 7.35 us -> 5.27 us
  other arithmetic: 1.53 us -> 0.15 us
  matrix products: 0.7 us -> 0 us
    ppermute x4 -> x0, starting transfers between devices: 9.01 us -> none  [the longest x2 6.43 us: neighbours(): low = lax.ppermute(last, axis, forward)]
    pallas_call x1, Pallas kernels: 26.4 us -> 33.7 us  [body(): pl.pallas_call(functools.partial(coarsen, n, ny, orders), out_shape=jax.S...]
    slice x2 -> x0, local copies, waits for them, and re-layouts: 1.88 us -> none  [the longest x1 0.95 us: neighbours(): first = lax.slice_in_dim(block, 0, 1, axis=dim)]
    another operation x6 -> x0, local copies, waits for them, and re-layouts: 1.75 us -> none  [body(): jnp.stack([prolong, jnp.concatenate([low_x, prolong[:-1]], axis=0), jnp.c...]
    unnamed x10, local copies, waits for them, and re-layouts: 1.49 us -> 3.18 us
    mul x2 -> x0, other arithmetic: 1.35 us -> none  [the longest x1 0.69 us: body(): owner_at[:, :, None] * CS + jnp.arange(CS, dtype=jnp.int32)[None, None, :]]
    dot_general x1 -> x0, matrix products: 0.7 us -> none  [body(): jnp.einsum('eba,ekbc->ekac', own_block, product, preferred_element_type=j...]
  transfers between devices with their start and end apart: 4 -> 0, of which waited for: 0 -> 0; matrix products, arithmetic and copies ran while one was open for 16% -> 0% of each run, Pallas kernels for 0% -> 0%
where the time goes in v2:
time: 39.4 us; the launch traced here: 39.2 us
  Pallas kernels  33.7 us (86%)
  local copies, waits for them, and re-layouts  5.27 us (13%)
    pallas_call x1, Pallas kernels, body(): pl.pallas_call(functools.partial(coarsen, n, ny, orders), out_shape=jax.S...  33.7 us
    unnamed x10, local copies, waits for them, and re-layouts  3.18 us

profile of v2, /device:TPU:0, one launch (start us, length us, event | category | flops | bytes accessed | tf_op | source)
XLA Modules:
  0.0 39.2 jit_solution(17658944017825031172)
XLA Ops:
  0.0 1.2 %copy.10 = bf16[1,8,5,4096]{3,2,1,0:T(8,128)(2,1)S(1)} copy(bf16[1,8,5,4096]{3,1,2,0:T(8,128)(2,1)} %param.5) | data formatting | bytes 655360 | tf_op args[0]
  1.2 0.0 copy-start
  1.2 0.7 %reshape.28.a_ref = bf16[40,64,64]{2,1,0:T(8,128)(2,1)S(1)} reshape(bf16[1,8,5,4096]{3,2,1,0:T(8,128)(2,1)S(1)} %copy.10) | data formatting | bytes 655360 | tf_op jit(solution)/shard_map/reshape | solution.py:169
  1.9 0.1 copy-done
  2.0 0.0 copy-start.1
  2.0 0.2 reshape.29.p_ref
  2.2 0.5 %copy-done.1 = s32[1,8,5]{1,0,2:T(1,128)S(1)} copy-done((s32[1,8,5]{1,0,2:T(1,128)S(1)}, s32[1,8,5]{1,0,2:T(1,128)}, u32[]{:S(2)}) %copy-start.1) | copy-done | bytes 184
  2.7 0.1 copy.9
  2.8 0.1 eq.38
  2.9 0.1 fusion
  2.9 0.1 reshape.33.slot_ref
  3.0 0.0 copy-start.2
  3.0 0.7 %copy-done.2 = s32[2,16]{1,0:T(2,128)S(1)} copy-done((s32[2,16]{1,0:T(2,128)S(1)}, s32[2,16]{1,0:T(2,128)}, u32[]{:S(2)}) %copy-start.2) | copy-done | bytes 152
  3.7 0.0 copy-start.3
  3.7 0.7 %copy-done.3 = s32[1,8]{1,0:T(1,128)S(1)} copy-done((s32[1,8]{1,0:T(1,128)S(1)}, s32[1,8]{1,0:T(1,128)}, u32[]{:S(2)}) %copy-start.3) | copy-done | bytes 56
  4.4 0.1 compare_convert_fusion
  4.4 0.1 reshape.32.owner_ref
  4.5 33.7 %shard_map.55 = f32[64,512]{1,0:T(8,128)S(1)} custom-call(f32[256]{0:T(256)S(1)} %reshape.32.owner_ref, f32[320]{0:T(512)S(1)} %reshape.33.slot_ref, bf16[40,64,64]{2,1,0:T(8,128)(2,1)S(1)} %reshape.28.a_ref, bf16[8,64,64]{2,1,0:T(8,128)(2,1)S(1)} %reshape.29.p_ref), custom_call_target="tpu_custom_call" | custom-call | tf_op jit(solution)/shard_map/pallas_call | solution.py:184
  38.2 0.1 reshape.30
  38.3 0.1 copy.11
  38.4 0.8 %reshape.31 = f32[1,1,8,4096]{3,2,1,0:T(8,128)} reshape(f32[8,64,64]{2,1,0:T(8,128)S(1)} %copy.11) | data formatting | bytes 262144 | tf_op jit(solution)/shard_map/reshape | solution.py:210
  (1 shorter events, 0.0 us)
Async XLA Ops:
  1.2 0.8 %copy-start = (bf16[1,8,4096]{2,1,0:T(8,128)(2,1)S(1)}, bf16[1,8,4096]{2,1,0:T(8,128)(2,1)}, u32[]{:S(2)}) copy-start(bf16[1,8,4096]{2,1,0:T(8,128)(2,1)} %param.6) | copy-start | bytes 196612
  2.0 0.7 %copy-start.1 = (s32[1,8,5]{1,0,2:T(1,128)S(1)}, s32[1,8,5]{1,0,2:T(1,128)}, u32[]{:S(2)}) copy-start(s32[1,8,5]{1,0,2:T(1,128)} %param.8) | copy-start | bytes 484
  3.0 0.7 %copy-start.2 = (s32[2,16]{1,0:T(2,128)S(1)}, s32[2,16]{1,0:T(2,128)}, u32[]{:S(2)}) copy-start(s32[2,16]{1,0:T(2,128)} %constant.8.clone) | copy-start | bytes 388
  3.7 0.7 %copy-start.3 = (s32[1,8]{1,0:T(1,128)S(1)}, s32[1,8]{1,0:T(1,128)}, u32[]{:S(2)}) copy-start(s32[1,8]{1,0:T(1,128)} %param.7) | copy-start | bytes 100

commit v3 on v2

--- a/solution.py
+++ b/solution.py
@@ -15,10 +15,8 @@
 
 def bit_orders(n):
     bits = [1 << i for i in range(n.bit_length() - 1)]
-    swapped = list(bits)
-    for i in range(0, len(bits) - 1, 2):
-        swapped[i], swapped[i + 1] = bits[i + 1], bits[i]
-    return bits, swapped
+    first = min(3, len(bits))
+    return [bits[i:first] + bits[:i] + bits[first:] for i in range(first)]
 
 
 def places(order):
@@ -30,13 +28,20 @@
 
 def coarsen(
     n, ny, orders, owner_ref, slot_ref, a_ref, p_ref, out_ref,
-    low_x, high_x, low_y, high_y, sums, parts, acc, *rest,
+    low_x, high_x, low_y, high_y, products, sums, parts, acc, *rest,
 ):
     steps = len(orders[0])
     send, recv = rest[:steps], rest[steps : 2 * steps]
     send_sem, recv_sem, halo_send, halo_recv = rest[2 * steps :]
     me, column = lax.axis_index("gx"), lax.axis_index("gy")
     elements = p_ref.shape[0]
+    chains = send[0].shape[0]
+    rows, width = send[0].shape[2:]
+    bands = p_ref.shape[1] // rows
+
+    def part_of(chain):
+        low, left = (chain % bands) * rows, (chain // bands) * width
+        return slice(low, low + rows), slice(left, left + width)
 
     def partner(bit):
         return me + bit - 2 * bit * ((me // bit) % 2)
@@ -77,26 +82,33 @@
         @pl.when(jnp.logical_not(receives))
         def _():
             place[...] = jnp.zeros_like(place)
+
+    def multiply(e, k, block):
+        products[e * K + k] = jnp.dot(
+            a_ref[e * K + k], block, preferred_element_type=jnp.float32
+        ).astype(jnp.bfloat16)
+
+    for e in range(elements):
+        multiply(e, 0, p_ref[e])
+        if e:
+            multiply(e, 3, p_ref[e - 1])
+        if e + 1 < elements:
+            multiply(e, 4, p_ref[e + 1])
     for i in range(4):
         @pl.when(sides[i][1])
         def _():
             halo(i).wait_recv()
+    multiply(0, 3, low_y[...])
+    multiply(elements - 1, 4, high_y[...])
 
     for e in range(elements):
-        beside = [
-            p_ref[e], low_x[e], high_x[e],
-            p_ref[e - 1] if e else low_y[...],
-            p_ref[e + 1] if e + 1 < elements else high_y[...],
-        ]
-        products = [
-            jnp.dot(a_ref[e * K + k], beside[k], preferred_element_type=jnp.float32)
-            .astype(jnp.bfloat16).astype(jnp.float32)
-            for k in range(K)
-        ]
+        multiply(e, 1, low_x[e])
+        multiply(e, 2, high_x[e])
+        terms = [products[e * K + k].astype(jnp.float32) for k in range(K)]
         for s in range(CS):
-            total = products[0] * slot_ref[(e * K) * CS + s]
+            total = terms[0] * jnp.where(slot_ref[e * K] == s, 1.0, 0.0)
             for k in range(1, K):
-                total = total + products[k] * slot_ref[(e * K + k) * CS + s]
+                total = total + terms[k] * jnp.where(slot_ref[e * K + k] == s, 1.0, 0.0)
             sums[e % 2, :, s * B : (s + 1) * B] = total.astype(jnp.bfloat16)
         parts[e] = (
             lax.dot_general(
@@ -105,13 +117,12 @@
             ).astype(jnp.bfloat16).astype(jnp.float32)
         )
 
-    rows = B // 2
-
     def gathered(chain, place):
-        base = (chain * n + place) * elements
-        total = parts[0, chain * rows : (chain + 1) * rows, :] * owner_ref[base]
+        band, lanes = part_of(chain)
+        base = (chain % len(orders) * n + place) * elements
+        total = parts[0, band, lanes] * owner_ref[base]
         for e in range(1, elements):
-            total = total + parts[e, chain * rows : (chain + 1) * rows, :] * owner_ref[base + e]
+            total = total + parts[e, band, lanes] * owner_ref[base + e]
         return total
 
     def copy(chain, step):
@@ -120,25 +131,25 @@
             dst_ref=recv[step].at[chain],
             send_sem=send_sem.at[chain, step],
             recv_sem=recv_sem.at[chain, step],
-            device_id={"gx": partner(orders[chain][step])},
+            device_id={"gx": partner(orders[chain % len(orders)][step])},
             device_id_type=MESH,
         )
 
     half = n // 2
-    for chain in range(2):
+    for chain in range(chains):
         @pl.loop(0, half)
         def _(p):
             send[0][chain, p] = gathered(chain, half + p).astype(jnp.bfloat16)
 
         copy(chain, 0).start()
-    for chain in range(2):
+    for chain in range(chains):
         @pl.loop(0, half)
         def _(p):
             acc[chain, p] = gathered(chain, p)
 
     for step in range(steps):
         count = half >> step
-        for chain in range(2):
+        for chain in range(chains):
             copy(chain, step).wait_recv()
             if step + 1 < steps:
                 keep = count // 2
@@ -150,11 +161,12 @@
                     jnp.float32
                 )
             else:
-                out_ref[chain * rows : (chain + 1) * rows, :] = acc[chain, 0] + recv[step][
+                band, lanes = part_of(chain)
+                out_ref[band, lanes] = acc[chain, 0] + recv[step][
                     chain, 0
                 ].astype(jnp.float32)
     for step in range(steps):
-        for chain in range(2):
+        for chain in range(chains):
             copy(chain, step).wait_send()
     for i in range(4):
         @pl.when(sides[i][0])
@@ -175,10 +187,10 @@
     owner_at = jnp.bitwise_xor(offsets, lax.axis_index("gx"))
     owners = aggregate.reshape(elements)
     owner_is = (owner_at[:, :, None] == owners[None, None, :]).astype(jnp.float32).reshape(-1)
-    slots = coupling_slot.reshape(elements * K, 1)
-    slot_is = (slots == jnp.arange(CS, dtype=jnp.int32)[None, :]).astype(jnp.float32).reshape(-1)
-
-    places_of = [(2, n >> (step + 1), B // 2, CS * B) for step in range(steps)]
+    slots = coupling_slot.reshape(elements * K)
+
+    chains = 8
+    places_of = [(chains, n >> (step + 1), B // 4, CS * B // 2) for step in range(steps)]
     vmem = pl.BlockSpec(memory_space=pltpu.VMEM)
     smem = pl.BlockSpec(memory_space=pltpu.SMEM)
     coarse = pl.pallas_call(
@@ -191,21 +203,22 @@
             pltpu.VMEM((elements, B, B), jnp.bfloat16),
             pltpu.VMEM((B, B), jnp.bfloat16),
             pltpu.VMEM((B, B), jnp.bfloat16),
+            pltpu.VMEM((elements * K, B, B), jnp.bfloat16),
             pltpu.VMEM((2, B, CS * B), jnp.bfloat16),
             pltpu.VMEM((elements, B, CS * B), jnp.float32),
             pltpu.VMEM(places_of[0], jnp.float32),
         ]
         + [pltpu.VMEM(shape, jnp.bfloat16) for shape in places_of + places_of]
         + [
-            pltpu.SemaphoreType.DMA((2, steps)),
-            pltpu.SemaphoreType.DMA((2, steps)),
+            pltpu.SemaphoreType.DMA((chains, steps)),
+            pltpu.SemaphoreType.DMA((chains, steps)),
             pltpu.SemaphoreType.DMA((4,)),
             pltpu.SemaphoreType.DMA((4,)),
         ],
         compiler_params=pltpu.CompilerParams(
             collective_id=0, has_side_effects=True, vmem_limit_bytes=40 * 1024 * 1024
         ),
-    )(owner_is, slot_is, matrix_a, matrix_p)
+    )(owner_is, slots, matrix_a, matrix_p)
     coarse = coarse.reshape(B, CS, B).transpose(1, 0, 2)
     return coarse.reshape(1, 1, CS, block_len)
 

time: 39.4 us -> 36.1 us (0.916)
  Pallas kernels: 33.7 us -> 30.5 us
    pallas_call x1, Pallas kernels: 33.7 us -> 30.5 us  [body(): pl.pallas_call(functools.partial(coarsen, n, ny, orders), out_shape=jax.S...]
where the time goes in v3:
time: 36.1 us; the launch traced here: 35.9 us
  Pallas kernels  30.5 us (84%)
  local copies, waits for them, and re-layouts  5.27 us (15%)
    pallas_call x1, Pallas kernels, body(): pl.pallas_call(functools.partial(coarsen, n, ny, orders), out_shape=jax.S...  30.5 us
    unnamed x10, local copies, waits for them, and re-layouts  3.28 us
    reshape x1, local copies, waits for them, and re-layouts, body(): return coarse.reshape(1, 1, CS, block_len)  0.77 us
    reshape x1, local copies, waits for them, and re-layouts, body(): matrix_a = blocks_a.reshape(elements * K, B, B)  0.72 us

profile of v3, /device:TPU:0, one launch (start us, length us, event | category | flops | bytes accessed | tf_op | source)
XLA Modules:
  0.0 35.9 jit_solution(10966126006801597010)
XLA Ops:
  0.0 1.2 %copy.10 = bf16[1,8,5,4096]{3,2,1,0:T(8,128)(2,1)S(1)} copy(bf16[1,8,5,4096]{3,1,2,0:T(8,128)(2,1)} %param.5) | data formatting | bytes 655360 | tf_op args[0]
  1.2 0.0 copy-start
  1.2 0.7 %reshape.24.a_ref = bf16[40,64,64]{2,1,0:T(8,128)(2,1)S(1)} reshape(bf16[1,8,5,4096]{3,2,1,0:T(8,128)(2,1)S(1)} %copy.10) | data formatting | bytes 655360 | tf_op jit(solution)/shard_map/reshape | solution.py:181
  1.9 0.1 copy-done
  2.0 0.2 reshape.25.p_ref
  2.2 0.0 copy-start.2
  2.2 0.7 %copy-done.2 = s32[3,16]{1,0:T(4,128)S(1)} copy-done((s32[3,16]{1,0:T(4,128)S(1)}, s32[3,16]{1,0:T(4,128)}, u32[]{:S(2)}) %copy-start.2) | copy-done | bytes 216
  2.9 0.0 copy-start.3
  2.9 0.7 %copy-done.3 = s32[1,8]{1,0:T(1,128)S(1)} copy-done((s32[1,8]{1,0:T(1,128)S(1)}, s32[1,8]{1,0:T(1,128)}, u32[]{:S(2)}) %copy-start.3) | copy-done | bytes 56
  3.5 0.1 compare_convert_fusion
  3.6 0.0 copy-start.1
  3.6 0.1 reshape.28.owner_ref
  3.7 0.6 %copy-done.1 = s32[1,8,5]{1,0,2:T(1,128)S(1)} copy-done((s32[1,8,5]{1,0,2:T(1,128)S(1)}, s32[1,8,5]{1,0,2:T(1,128)}, u32[]{:S(2)}) %copy-start.1) | copy-done | bytes 184
  4.3 0.1 copy.9
  4.4 0.1 reshape.23.slot_ref
  4.5 30.5 %shard_map.55 = f32[64,512]{1,0:T(8,128)S(1)} custom-call(f32[384]{0:T(512)S(1)} %reshape.28.owner_ref, s32[40]{0:T(128)S(1)} %reshape.23.slot_ref, bf16[40,64,64]{2,1,0:T(8,128)(2,1)S(1)} %reshape.24.a_ref, bf16[8,64,64]{2,1,0:T(8,128)(2,1)S(1)} %reshape.25.p_ref), custom_call_target="tpu_custom_call" | custom-call | tf_op jit(solution)/shard_map/pallas_call | solution.py:196
  34.9 0.1 reshape.26
  35.0 0.1 copy.11
  35.1 0.8 %reshape.27 = f32[1,1,8,4096]{3,2,1,0:T(8,128)} reshape(f32[8,64,64]{2,1,0:T(8,128)S(1)} %copy.11) | data formatting | bytes 262144 | tf_op jit(solution)/shard_map/reshape | solution.py:223
  (1 shorter events, 0.0 us)
Async XLA Ops:
  1.2 0.8 %copy-start = (bf16[1,8,4096]{2,1,0:T(8,128)(2,1)S(1)}, bf16[1,8,4096]{2,1,0:T(8,128)(2,1)}, u32[]{:S(2)}) copy-start(bf16[1,8,4096]{2,1,0:T(8,128)(2,1)} %param.6) | copy-start | bytes 196612
  2.2 0.7 %copy-start.2 = (s32[3,16]{1,0:T(4,128)S(1)}, s32[3,16]{1,0:T(4,128)}, u32[]{:S(2)}) copy-start(s32[3,16]{1,0:T(4,128)} %constant.8.clone) | copy-start | bytes 580
  2.9 0.7 %copy-start.3 = (s32[1,8]{1,0:T(1,128)S(1)}, s32[1,8]{1,0:T(1,128)}, u32[]{:S(2)}) copy-start(s32[1,8]{1,0:T(1,128)} %param.7) | copy-start | bytes 100
  3.6 0.7 %copy-start.1 = (s32[1,8,5]{1,0,2:T(1,128)S(1)}, s32[1,8,5]{1,0,2:T(1,128)}, u32[]{:S(2)}) copy-start(s32[1,8,5]{1,0,2:T(1,128)} %param.8) | copy-start | bytes 484

commit v4 on v3

--- a/solution.py
+++ b/solution.py
@@ -19,10 +19,14 @@
     return [bits[i:first] + bits[:i] + bits[first:] for i in range(first)]
 
 
-def places(order):
-    offsets = [0]
-    for bit in reversed(order):
-        offsets = offsets + [o | bit for o in offsets]
+def places(orders, n):
+    which = lax.broadcasted_iota(jnp.int32, (len(orders), n), 0)
+    place = lax.broadcasted_iota(jnp.int32, (len(orders), n), 1)
+    offsets = jnp.zeros_like(place)
+    for i, order in enumerate(orders):
+        for step, bit in enumerate(order):
+            on = (place >> (len(order) - 1 - step)) & 1
+            offsets = offsets + jnp.where(which == i, on * bit, 0)
     return offsets
 
 
@@ -85,7 +89,7 @@
 
     def multiply(e, k, block):
         products[e * K + k] = jnp.dot(
-            a_ref[e * K + k], block, preferred_element_type=jnp.float32
+            a_ref[k * elements + e], block, preferred_element_type=jnp.float32
         ).astype(jnp.bfloat16)
 
     for e in range(elements):
@@ -106,9 +110,9 @@
         multiply(e, 2, high_x[e])
         terms = [products[e * K + k].astype(jnp.float32) for k in range(K)]
         for s in range(CS):
-            total = terms[0] * jnp.where(slot_ref[e * K] == s, 1.0, 0.0)
+            total = terms[0] * jnp.where(slot_ref[e] == s, 1.0, 0.0)
             for k in range(1, K):
-                total = total + terms[k] * jnp.where(slot_ref[e * K + k] == s, 1.0, 0.0)
+                total = total + terms[k] * jnp.where(slot_ref[k * elements + e] == s, 1.0, 0.0)
             sums[e % 2, :, s * B : (s + 1) * B] = total.astype(jnp.bfloat16)
         parts[e] = (
             lax.dot_general(
@@ -137,13 +141,13 @@
 
     half = n // 2
     for chain in range(chains):
-        @pl.loop(0, half)
+        @pl.loop(0, half, unroll=4)
         def _(p):
             send[0][chain, p] = gathered(chain, half + p).astype(jnp.bfloat16)
 
         copy(chain, 0).start()
     for chain in range(chains):
-        @pl.loop(0, half)
+        @pl.loop(0, half, unroll=4)
         def _(p):
             acc[chain, p] = gathered(chain, p)
 
@@ -178,16 +182,16 @@
     grid_rows, grid_cols, block_len = prolong.shape
     elements = grid_rows * grid_cols
     n, ny = lax.axis_size("gx"), lax.axis_size("gy")
-    matrix_a = blocks_a.reshape(elements * K, B, B)
+    matrix_a = blocks_a.transpose(2, 0, 1, 3).reshape(K * elements, B, B)
     matrix_p = prolong.reshape(elements, B, B)
 
     orders = bit_orders(n)
     steps = len(orders[0])
-    offsets = jnp.asarray([places(order) for order in orders], jnp.int32)
+    offsets = places(orders, n)
     owner_at = jnp.bitwise_xor(offsets, lax.axis_index("gx"))
     owners = aggregate.reshape(elements)
     owner_is = (owner_at[:, :, None] == owners[None, None, :]).astype(jnp.float32).reshape(-1)
-    slots = coupling_slot.reshape(elements * K)
+    slots = coupling_slot.transpose(2, 0, 1).reshape(K * elements)
 
     chains = 8
     places_of = [(chains, n >> (step + 1), B // 4, CS * B // 2) for step in range(steps)]

time: 36.1 us -> 35 us (0.970)
  local copies, waits for them, and re-layouts: 5.27 us -> 3.99 us
    unnamed x10 -> x6, local copies, waits for them, and re-layouts: 3.28 us -> 1.09 us
    reshape x2, local copies, waits for them, and re-layouts: 0.81 us -> 1.7 us  [the longest x1 1.62 us: body(): matrix_a = blocks_a.transpose(2, 0, 1, 3).reshape(K * elements, B, B)]
where the time goes in v4:
time: 35 us; the launch traced here: 34.8 us
  Pallas kernels  30.5 us (87%)
  local copies, waits for them, and re-layouts  3.99 us (11%)
    pallas_call x1, Pallas kernels, body(): pl.pallas_call(functools.partial(coarsen, n, ny, orders), out_shape=jax.S...  30.5 us
    reshape x1, local copies, waits for them, and re-layouts, body(): matrix_a = blocks_a.transpose(2, 0, 1, 3).reshape(K * elements, B, B)  1.62 us
    unnamed x6, local copies, waits for them, and re-layouts  1.09 us
    reshape x1, local copies, waits for them, and re-layouts, body(): return coarse.reshape(1, 1, CS, block_len)  0.77 us

profile of v4, /device:TPU:0, one launch (start us, length us, event | category | flops | bytes accessed | tf_op | source)
XLA Modules:
  0.0 34.8 jit_solution(13154367493806314500)
XLA Ops:
  0.0 0.0 copy-start
  0.0 0.0 copy-start.1
  0.1 0.1 add_xor_fusion
  0.2 0.5 %copy-done = s32[1,8,5]{1,0,2:T(1,128)S(1)} copy-done((s32[1,8,5]{1,0,2:T(1,128)S(1)}, s32[1,8,5]{1,0,2:T(1,128)}, u32[]{:S(2)}) %copy-start) | copy-done | bytes 184
  0.7 0.0 copy-start.2
  0.7 0.1 reshape.294.slot_ref
  0.8 0.6 %copy-done.2 = s32[1,8]{1,0:T(1,128)S(1)} copy-done((s32[1,8]{1,0:T(1,128)S(1)}, s32[1,8]{1,0:T(1,128)}, u32[]{:S(2)}) %copy-start.2) | copy-done | bytes 56
  1.4 0.1 compare_convert_fusion
  1.4 0.1 reshape.299.owner_ref
  1.5 0.0 copy-done.1
  1.5 0.2 reshape.296.p_ref
  1.7 1.6 %reshape.295.a_ref = bf16[40,64,64]{2,1,0:T(8,128)(2,1)S(1)} reshape(bf16[5,1,8,4096]{3,2,0,1:T(8,128)(2,1)} %bitcast.10) | data formatting | bytes 655360 | tf_op jit(solution)/shard_map/reshape | solution.py:185
  3.3 30.5 %shard_map.46 = f32[64,512]{1,0:T(8,128)S(1)} custom-call(f32[384]{0:T(512)S(1)} %reshape.299.owner_ref, s32[40]{0:T(128)S(1)} %reshape.294.slot_ref, bf16[40,64,64]{2,1,0:T(8,128)(2,1)S(1)} %reshape.295.a_ref, bf16[8,64,64]{2,1,0:T(8,128)(2,1)S(1)} %reshape.296.p_ref), custom_call_target="tpu_custom_call" | custom-call | tf_op jit(solution)/shard_map/pallas_call | solution.py:200
  33.8 0.1 reshape.297
  33.9 0.1 copy.6
  34.0 0.8 %reshape.298 = f32[1,1,8,4096]{3,2,1,0:T(8,128)} reshape(f32[8,64,64]{2,1,0:T(8,128)S(1)} %copy.6) | data formatting | bytes 262144 | tf_op jit(solution)/shard_map/reshape | solution.py:227
  (8 shorter events, 0.1 us)
Async XLA Ops:
  0.0 0.7 %copy-start = (s32[1,8,5]{1,0,2:T(1,128)S(1)}, s32[1,8,5]{1,0,2:T(1,128)}, u32[]{:S(2)}) copy-start(s32[1,8,5]{1,0,2:T(1,128)} %param.7) | copy-start | bytes 484
  0.0 1.5 %copy-start.1 = (bf16[1,8,4096]{2,1,0:T(8,128)(2,1)S(1)}, bf16[1,8,4096]{2,1,0:T(8,128)(2,1)}, u32[]{:S(2)}) copy-start(bf16[1,8,4096]{2,1,0:T(8,128)(2,1)} %param.5) | copy-start | bytes 196612
  0.7 0.7 %copy-start.2 = (s32[1,8]{1,0:T(1,128)S(1)}, s32[1,8]{1,0:T(1,128)}, u32[]{:S(2)}) copy-start(s32[1,8]{1,0:T(1,128)} %param.6) | copy-start | bytes 100

commit v5 on v4

--- a/solution.py
+++ b/solution.py
@@ -161,14 +161,17 @@
                     acc[chain, keep:count] + recv[step][chain, keep:count].astype(jnp.float32)
                 ).astype(jnp.bfloat16)
                 copy(chain, step + 1).start()
-                acc[chain, 0:keep] = acc[chain, 0:keep] + recv[step][chain, 0:keep].astype(
-                    jnp.float32
-                )
             else:
                 band, lanes = part_of(chain)
                 out_ref[band, lanes] = acc[chain, 0] + recv[step][
                     chain, 0
                 ].astype(jnp.float32)
+        if step + 1 < steps:
+            keep = count // 2
+            for chain in range(chains):
+                acc[chain, 0:keep] = acc[chain, 0:keep] + recv[step][chain, 0:keep].astype(
+                    jnp.float32
+                )
     for step in range(steps):
         for chain in range(chains):
             copy(chain, step).wait_send()

time: 35 us -> 35 us (level)
  no operation moved by 1% of the time
where the time goes in v5:
time: 35 us; the launch traced here: 34.8 us
  Pallas kernels  30.5 us (87%)
  local copies, waits for them, and re-layouts  3.99 us (11%)
    pallas_call x1, Pallas kernels, body(): pl.pallas_call(functools.partial(coarsen, n, ny, orders), out_shape=jax.S...  30.5 us
    reshape x1, local copies, waits for them, and re-layouts, body(): matrix_a = blocks_a.transpose(2, 0, 1, 3).reshape(K * elements, B, B)  1.62 us
    unnamed x6, local copies, waits for them, and re-layouts  1.09 us
    reshape x1, local copies, waits for them, and re-layouts, body(): return coarse.reshape(1, 1, CS, block_len)  0.77 us

profile of v5, /device:TPU:0, one launch (start us, length us, event | category | flops | bytes accessed | tf_op | source)
XLA Modules:
  0.0 34.8 jit_solution(8634289992633724377)
XLA Ops:
  0.0 0.0 copy-start
  0.0 0.0 copy-start.1
  0.1 0.1 add_xor_fusion
  0.2 0.5 %copy-done = s32[1,8,5]{1,0,2:T(1,128)S(1)} copy-done((s32[1,8,5]{1,0,2:T(1,128)S(1)}, s32[1,8,5]{1,0,2:T(1,128)}, u32[]{:S(2)}) %copy-start) | copy-done | bytes 184
  0.7 0.0 copy-start.2
  0.7 0.1 reshape.294.slot_ref
  0.8 0.6 %copy-done.2 = s32[1,8]{1,0:T(1,128)S(1)} copy-done((s32[1,8]{1,0:T(1,128)S(1)}, s32[1,8]{1,0:T(1,128)}, u32[]{:S(2)}) %copy-start.2) | copy-done | bytes 56
  1.4 0.1 compare_convert_fusion
  1.4 0.1 reshape.299.owner_ref
  1.5 0.0 copy-done.1
  1.5 0.2 reshape.296.p_ref
  1.7 1.6 %reshape.295.a_ref = bf16[40,64,64]{2,1,0:T(8,128)(2,1)S(1)} reshape(bf16[5,1,8,4096]{3,2,0,1:T(8,128)(2,1)} %bitcast.10) | data formatting | bytes 655360 | tf_op jit(solution)/shard_map/reshape | solution.py:188
  3.3 30.5 %shard_map.46 = f32[64,512]{1,0:T(8,128)S(1)} custom-call(f32[384]{0:T(512)S(1)} %reshape.299.owner_ref, s32[40]{0:T(128)S(1)} %reshape.294.slot_ref, bf16[40,64,64]{2,1,0:T(8,128)(2,1)S(1)} %reshape.295.a_ref, bf16[8,64,64]{2,1,0:T(8,128)(2,1)S(1)} %reshape.296.p_ref), custom_call_target="tpu_custom_call" | custom-call | tf_op jit(solution)/shard_map/pallas_call | solution.py:203
  33.8 0.1 reshape.297
  33.9 0.1 copy.6
  34.0 0.8 %reshape.298 = f32[1,1,8,4096]{3,2,1,0:T(8,128)} reshape(f32[8,64,64]{2,1,0:T(8,128)S(1)} %copy.6) | data formatting | bytes 262144 | tf_op jit(solution)/shard_map/reshape | solution.py:230
  (8 shorter events, 0.1 us)
Async XLA Ops:
  0.0 0.7 %copy-start = (s32[1,8,5]{1,0,2:T(1,128)S(1)}, s32[1,8,5]{1,0,2:T(1,128)}, u32[]{:S(2)}) copy-start(s32[1,8,5]{1,0,2:T(1,128)} %param.7) | copy-start | bytes 484
  0.0 1.5 %copy-start.1 = (bf16[1,8,4096]{2,1,0:T(8,128)(2,1)S(1)}, bf16[1,8,4096]{2,1,0:T(8,128)(2,1)}, u32[]{:S(2)}) copy-start(bf16[1,8,4096]{2,1,0:T(8,128)(2,1)} %param.5) | copy-start | bytes 196612
  0.7 0.7 %copy-start.2 = (s32[1,8]{1,0:T(1,128)S(1)}, s32[1,8]{1,0:T(1,128)}, u32[]{:S(2)}) copy-start(s32[1,8]{1,0:T(1,128)} %param.6) | copy-start | bytes 100
